TPU v7x, 32 devices: a whole 2x2x4 slice. The times are simulated.
32 devices in a mesh: grp: 2 (over y), wide: 16 (over z, x, core).
Axes of the slice: x: 2, y: 2, z: 4, core: 2. Of those that a mesh axis runs over, the one named last changes fastest.
Arguments:
- year_slab: bfloat16 [1024, 4096], P(('grp', 'wide')), parts along dimension 0, may hold values from -12 to 12
- harmonic_fit: float32 [21, 4096], P(None, 'wide'), may hold values from -6 to 6
- patterns: bfloat16 [4096, 256], P('wide'), may hold values from -0.09375 to 0.09375
- reader_table: int32 [16], replicated, may hold values from 0 to 15, each once
- land_mask: int32 [4096], P('wide'), may hold values 0 or 1
Outputs:
- components: float32 [1024, 256], P(('grp', 'wide')), parts along dimension 0
There are 2 independent parts, one for each index of `grp`. A program takes and returns all parts, laid end to end along the dimension named above; an argument that names none is the same for every part. Nothing has to cross between parts.
Inputs may be any that keep to these rules, and one draw needn't show every extreme that they name: `reader_table`: each of the 16 groups is held by exactly one reader.
All inputs are finite; a program needn't handle non-finite values. No bound on the sum of `land_mask` on one device may be relied on, other than what follows from the above.
Results may differ from a plain program's by a relative error of at most 0.0029.
Values may be sent and summed in bfloat16 or wider, within the bound.
A program may use at most 64 MiB of HBM per device.

v0:
```python
import math

import jax
import jax.numpy as jnp
from jax import lax
from jax.sharding import PartitionSpec as P

NHARM = 8
NDIUR = 2


def regressors(hours, period):
    orders = jnp.arange(1, NHARM + 1, dtype=jnp.int32)
    slow = (hours[..., None] * orders % period).astype(jnp.float32) * (2.0 * math.pi / period)
    daily_orders = jnp.arange(1, NDIUR + 1, dtype=jnp.int32)
    daily = (hours[..., None] * daily_orders % 24).astype(jnp.float32) * (2.0 * math.pi / 24.0)
    ones = jnp.ones(hours.shape + (1,), jnp.float32)
    return jnp.concatenate([ones, jnp.cos(slow), jnp.sin(slow), jnp.cos(daily), jnp.sin(daily)], -1)


def effective(harmonic_fit, land_mask):
    split = 1 + 2 * NHARM
    land = land_mask.astype(jnp.float32)[None, :]
    return jnp.concatenate([harmonic_fit[:split], harmonic_fit[split:] * land], 0)


def local(year_slab, harmonic_fit, patterns, reader_table, land_mask):
    readers = lax.axis_size("wide")
    group_rows = year_slab.shape[0]
    columns = patterns.shape[0]
    coeffs = effective(harmonic_fit, land_mask)
    arranged = year_slab.reshape(group_rows, readers, columns)
    received = lax.all_to_all(arranged, "wide", split_axis=1, concat_axis=1, tiled=True)
    hours = reader_table[None, :] * group_rows + jnp.arange(group_rows, dtype=jnp.int32)[:, None]
    design = regressors(hours, readers * group_rows)
    fitted = jnp.einsum("rsc,cp->rsp", design, coeffs, precision=lax.Precision.HIGHEST)
    anomaly = (received.astype(jnp.float32) - fitted).astype(jnp.bfloat16)
    partial_terms = jnp.einsum("rsp,pk->rsk", anomaly, patterns, preferred_element_type=jnp.float32)
    summed = lax.psum_scatter(partial_terms, "wide", scatter_dimension=1, tiled=True)
    components = summed.reshape(group_rows, partial_terms.shape[2])
    return components


def solution(mesh):
    placed = (P(("grp", "wide"), None), P(None, "wide"), P("wide", None), P(), P("wide"))
    return jax.shard_map(
        local, mesh=mesh, in_specs=placed, out_specs=P(("grp", "wide"), None), check_vma=False
    )
```

profile of v0, /device:TPU:0, one launch (start us, length us, event | category | flops | bytes accessed | tf_op | source)
XLA Modules:
  0.0 88.4 jit_solution(2735395090471878994)
XLA Ops:
  6.5 0.0 copy-start
  6.5 1.7 %copy.20 = bf16[4,16,8,256]{3,2,0,1:T(8,128)(2,1)} copy(bf16[4,16,8,256]{3,2,1,0:T(8,128)(2,1)} %bitcast.14) | data formatting | bytes 524288 | tf_op jit(solution)/shard_map/reshape | solution.py:32
  8.2 7.4 %all-to-all-start = ((bf16[32,16,256]{2,0,1:T(8,128)(2,1)}), bf16[32,16,256]{2,0,1:T(8,128)(2,1)S(1)}, u32[]{:S(2)}, u32[]{:S(2)}) async-start(bf16[32,16,256]{2,0,1:T(8,128)(2,1)} %bitcast.12), calls=%async_computation | async-start | bytes 524288 | tf_op jit(solution)/shard_map/all_to_all | solution.py:33
  15.6 0.0 copy-start.3
  15.6 0.0 reduce-scatter.2.cloned.1.call-start
  15.7 0.6 copy-done.3
  16.3 0.1 iota_add_fusion
  16.3 0.2 fusion.14
  16.5 0.0 copy-start.2
  16.5 0.7 copy-done.2
  17.2 0.3 fusion.6
  17.6 0.0 copy-start.1
  17.6 0.3 concatenate.6
  17.9 0.4 copy-done.1
  18.3 7.3 %all-to-all-done = bf16[32,16,256]{2,0,1:T(8,128)(2,1)S(1)} async-done(((bf16[32,16,256]{2,0,1:T(8,128)(2,1)}), bf16[32,16,256]{2,0,1:T(8,128)(2,1)S(1)}, u32[]{:S(2)}, u32[]{:S(2)}) %all-to-all-start) | async-done | bytes 262176 | tf_op jit(solution)/shard_map/all_to_all | solution.py:33
  25.7 0.6 fusion
  26.3 0.0 copy-done
  26.3 1.0 %fusion.1 = f32[32,16,256]{2,0,1:T(8,128)} fusion(bf16[32,16,256]{2,0,1:T(8,128)(2,1)S(1)} %fusion, bf16[256,256]{1,0:T(8,128)(2,1)S(1)} %copy-done), kind=kOutput, calls=%fused_computation.3 | convolution fusion | flops 67108864 | bytes 917504 | tf_op jit(solution)/shard_map/rsp,pk->rsk/dot_general | solution.py:38
  27.3 0.0 reduce-scatter.2.cloned.1.call-update
  27.4 54.2 %reduce-scatter.2.cloned.1.call-done = f32[32,1,256]{2,0,1:T(8,128)} async-done(((f32[32,16,256]{2,0,1:T(8,128)}), f32[32,1,256]{2,0,1:T(8,128)}) %reduce-scatter.2.cloned.1.call-update) | async-done | bytes 32784 | tf_op jit(solution)/shard_map/reduce_scatter | solution.py:39
  (8 shorter events, 0.0 us)
Async XLA Ops:
  6.5 19.8 %copy-start = (bf16[256,256]{1,0:T(8,128)(2,1)S(1)}, bf16[256,256]{1,0:T(8,128)(2,1)}, u32[]{:S(2)}) copy-start(bf16[256,256]{1,0:T(8,128)(2,1)} %param.7) | copy-start | bytes 393220
  8.2 17.4 %all-to-all-start = ((bf16[32,16,256]{2,0,1:T(8,128)(2,1)}), bf16[32,16,256]{2,0,1:T(8,128)(2,1)S(1)}, u32[]{:S(2)}, u32[]{:S(2)}) async-start(bf16[32,16,256]{2,0,1:T(8,128)(2,1)} %bitcast.12), calls=%async_computation | async-start | bytes 524288 | tf_op jit(solution)/shard_map/all_to_all | solution.py:33
  15.6 0.7 copy-start.3
  15.6 66.0 %reduce-scatter.2.cloned.1.call-start = ((), (), s32[]{:S(2)}) async-start(), calls=%async_computation.2 | async-start | bytes 557056 | tf_op jit(solution)/shard_map/reduce_scatter | solution.py:39
  16.5 0.7 copy-start.2
  17.6 0.7 copy-start.1
Sparse Core Ops, SparseCore 0:
  27.5 54.0 reduce-scatter.1
where the time goes:
time: 88.7 us; the launch traced here: 88.4 us
  waiting for transfers between devices  61.6 us (69%)
  between operations  13.5 us (15%)
  starting transfers between devices  7.4 us (8%)
  local copies, waits for them, and re-layouts  3.72 us (4%)
  matrix products  1.67 us (2%)
    reduce_scatter x1, waiting for transfers between devices, local(): lax.psum_scatter(partial_terms, 'wide', scatter_dimension=1, tiled=True)  54.2 us
    all_to_all x1, starting transfers between devices, local(): lax.all_to_all(arranged, 'wide', split_axis=1, concat_axis=1, tiled=True)  7.36 us
    all_to_all x1, waiting for transfers between devices, local(): lax.all_to_all(arranged, 'wide', split_axis=1, concat_axis=1, tiled=True)  7.33 us
  transfers between devices with their start and end apart: 2, of which 2 were waited for; matrix products, arithmetic and copies ran while one was open for 1% of the time, Pallas kernels for 0%

commit v1 on v0

v1 whole, which is shorter than its diff:
```python
import functools
import math

import jax
import jax.numpy as jnp
from jax import lax
from jax.experimental import pallas as pl
from jax.experimental.pallas import tpu as pltpu
from jax.sharding import PartitionSpec as P

NHARM = 8
NDIUR = 2
SPLIT = 1 + 2 * NHARM
LANES = 4
F32 = jnp.float32
BF16 = jnp.bfloat16


def thirds(value):
    first = value.astype(BF16)
    rest = value - first.astype(F32)
    second = rest.astype(BF16)
    third = (rest - second.astype(F32)).astype(BF16)
    return first, second, third


def design_terms(hour, period):
    shape = (hour.shape[0], 128)
    lane = lax.broadcasted_iota(jnp.int32, shape, 1)
    j = lane & 31
    hour = jnp.broadcast_to(hour, shape)
    slow_sine = (j > NHARM).astype(jnp.int32)
    slow_order = j - NHARM * slow_sine
    slow = (hour * slow_order + slow_sine * (3 * period // 4)) & (period - 1)
    slow_angle = slow.astype(F32) * (2.0 * math.pi / period)
    i = j - SPLIT
    daily_sine = (i >= NDIUR).astype(jnp.int32)
    daily_order = i + 1 - NDIUR * daily_sine
    daily = (hour * daily_order + daily_sine * 18).astype(F32)
    daily = daily - 24.0 * jnp.floor((daily + 0.5) * (1.0 / 24.0))
    daily_angle = daily * (2.0 * math.pi / 24.0)
    angle = jnp.where(j == 0, 0.0, jnp.where(j < SPLIT, slow_angle, daily_angle))
    value = jnp.where(j < SPLIT + 2 * NDIUR, jnp.cos(angle), 0.0)
    first = value.astype(BF16).astype(F32)
    rest = value - first
    second = rest.astype(BF16).astype(F32)
    third = rest - second
    low = jnp.where(lane < 96, first, second)
    high = jnp.where(lane < 32, second, jnp.where(lane < 64, third, 0.0))
    return low.astype(BF16), high.astype(BF16)


def kernel(
    planes, table_ref, y_ref, c_ref, p_ref, mask_ref, out_ref,
    craw, mraw, cbuf, cstack, pbuf, ybuf, fit, design, sbuf, rbuf,
    local_sem, plane_send, plane_recv, y_send, y_recv, r_send, r_recv,
):
    rows, wide_columns = ybuf.shape[1:]
    columns = p_ref.shape[0]
    period = planes * LANES * rows
    me = lax.axis_index("wide")
    plane, lane = me // LANES, me % LANES
    side = me - lane + (lane + 2) % LANES
    core = me + 1 - 2 * (lane % 2)

    def at_plane(offset):
        return ((plane + offset + planes) % planes) * LANES + lane

    def block(which):
        return pl.ds(pl.multiple_of(which * columns, columns), columns)

    c_in = pltpu.make_async_copy(c_ref, craw, local_sem.at[0])
    m_in = pltpu.make_async_copy(mask_ref, mraw, local_sem.at[1])
    p_in = pltpu.make_async_copy(p_ref, pbuf.at[block(lane)], local_sem.at[2])
    here = pl.ds(pl.multiple_of(plane * wide_columns, wide_columns), wide_columns)
    y_in = pltpu.make_async_copy(y_ref.at[:, here], ybuf.at[0], local_sem.at[3])
    c_in.start()
    m_in.start()
    p_in.start()
    y_in.start()

    barrier = pltpu.get_barrier_semaphore()
    peers = [side, core] + [at_plane(d) for d in range(1, planes)]
    for peer in peers:
        pl.semaphore_signal(barrier, inc=1, device_id={"wide": peer}, device_id_type=pl.DeviceIdType.MESH)

    c_in.wait()
    m_in.wait()
    coeff_row = lax.broadcasted_iota(jnp.int32, craw.shape, 0)
    land = mraw[...].astype(F32)
    cbuf[lane] = jnp.zeros(cbuf.shape[1:], F32)
    cbuf[lane, 0:craw.shape[0], :] = craw[...] * jnp.where(coeff_row < SPLIT, 1.0, land)

    pl.semaphore_wait(barrier, len(peers))

    def remote(src, dst, send_sem, recv_sem, peer):
        return pltpu.make_async_remote_copy(
            src_ref=src, dst_ref=dst, send_sem=send_sem, recv_sem=recv_sem,
            device_id={"wide": peer}, device_id_type=pl.DeviceIdType.MESH,
        )

    p_side = remote(p_ref, pbuf.at[block(lane)], plane_send.at[0], plane_recv.at[0], side)
    c_side = remote(cbuf.at[lane], cbuf.at[lane], plane_send.at[1], plane_recv.at[1], side)
    p_core = remote(p_ref, pbuf.at[block(lane)], plane_send.at[2], plane_recv.at[2], core)
    c_core = remote(cbuf.at[lane], cbuf.at[lane], plane_send.at[3], plane_recv.at[3], core)
    other = (lane + 2) % LANES
    p_on = remote(pbuf.at[block(other)], pbuf.at[block(other)], plane_send.at[4], plane_recv.at[4], core)
    c_on = remote(cbuf.at[other], cbuf.at[other], plane_send.at[5], plane_recv.at[5], core)
    y_out = []
    for d in range(1, planes):
        to = (plane + d) % planes
        there = pl.ds(pl.multiple_of(to * wide_columns, wide_columns), wide_columns)
        y_out.append(remote(y_ref.at[:, there], ybuf.at[d], y_send.at[d], y_recv.at[d], at_plane(d)))
    c_side.start()
    for copy in y_out:
        copy.start()
    p_side.start()
    c_core.start()
    p_core.start()

    row = lax.broadcasted_iota(jnp.int32, (rows, 1), 0)
    for d in range(planes):
        hour = table_ref[at_plane(-d)] * rows + row
        low, high = design_terms(hour, period)
        design[d * rows:(d + 1) * rows, 0:128] = low
        design[d * rows:(d + 1) * rows, 128:256] = high
    cstack[...] = jnp.zeros(cstack.shape, BF16)

    c_side.wait_recv()
    c_on.start()
    c_core.wait_recv()
    p_side.wait_recv()
    p_on.start()
    c_on.wait_recv()
    zeros = jnp.zeros((8, columns), F32)
    for l in range(LANES):
        c1, c2, c3 = thirds(jnp.concatenate([cbuf[l], zeros], 0))
        at = slice(l * columns, (l + 1) * columns)
        for place, term in enumerate((c1, c2, c3, c1, c2, c1)):
            cstack[place * 32:(place + 1) * 32, at] = term
    fit[...] = jnp.dot(design[...], cstack[...], preferred_element_type=F32)

    p_in.wait()
    p_core.wait_recv()
    p_on.wait_recv()

    def project(d):
        anomaly = ybuf[d].astype(F32) - fit[d * rows:(d + 1) * rows, :]
        return jnp.dot(anomaly.astype(BF16), pbuf[...], preferred_element_type=F32)

    y_in.wait()
    total = project(0)
    r_out = []
    for d in range(1, planes):
        y_out[d - 1].wait_recv()
        sbuf[d] = project(d).astype(sbuf.dtype)
        copy = remote(sbuf.at[d], rbuf.at[d], r_send.at[d], r_recv.at[d], at_plane(-d))
        copy.start()
        r_out.append(copy)
    for d in range(1, planes):
        r_out[d - 1].wait_recv()
        total = total + rbuf[d].astype(F32)
    out_ref[...] = total
    for copy in [p_side, c_side, p_core, c_core, p_on, c_on] + y_out + r_out:
        copy.wait_send()


def local(year_slab, harmonic_fit, patterns, reader_table, land_mask):
    readers = lax.axis_size("wide")
    planes = readers // LANES
    rows = year_slab.shape[0]
    columns, patterns_held = patterns.shape
    wide_columns = LANES * columns
    hbm = pl.BlockSpec(memory_space=pl.ANY)
    return pl.pallas_call(
        functools.partial(kernel, planes),
        out_shape=jax.ShapeDtypeStruct((rows, patterns_held), F32),
        in_specs=[pl.BlockSpec(memory_space=pltpu.SMEM), hbm, hbm, hbm, hbm],
        out_specs=pl.BlockSpec(memory_space=pltpu.VMEM),
        scratch_shapes=[
            pltpu.VMEM(harmonic_fit.shape, F32),
            pltpu.VMEM((1, columns), jnp.int32),
            pltpu.VMEM((LANES, 24, columns), F32),
            pltpu.VMEM((256, wide_columns), BF16),
            pltpu.VMEM((wide_columns, patterns_held), BF16),
            pltpu.VMEM((planes, rows, wide_columns), BF16),
            pltpu.VMEM((planes * rows, wide_columns), F32),
            pltpu.VMEM((planes * rows, 256), BF16),
            pltpu.VMEM((planes, rows, patterns_held), BF16),
            pltpu.VMEM((planes, rows, patterns_held), BF16),
            pltpu.SemaphoreType.DMA((4,)),
            pltpu.SemaphoreType.DMA((6,)),
            pltpu.SemaphoreType.DMA((6,)),
            pltpu.SemaphoreType.DMA((planes,)),
            pltpu.SemaphoreType.DMA((planes,)),
            pltpu.SemaphoreType.DMA((planes,)),
            pltpu.SemaphoreType.DMA((planes,)),
        ],
        compiler_params=pltpu.CompilerParams(
            collective_id=0, has_side_effects=True, vmem_limit_bytes=63 * 1024 * 1024 + 900 * 1024
        ),
        cost_estimate=pl.CostEstimate(
            flops=2 * planes * rows * wide_columns * (patterns_held + 256),
            bytes_accessed=2 * rows * readers * columns + 2 * columns * patterns_held,
            transcendentals=0,
        ),
    )(reader_table, year_slab, harmonic_fit, patterns, land_mask.reshape(1, columns))


def solution(mesh):
    placed = (P(("grp", "wide"), None), P(None, "wide"), P("wide", None), P(), P("wide"))
    return jax.shard_map(
        local, mesh=mesh, in_specs=placed, out_specs=P(("grp", "wide"), None), check_vma=False
    )
```

time: 88.7 us -> 19.6 us (0.22)
  waiting for transfers between devices: 61.6 us -> 0 us
  Pallas kernels: 0 us -> 18.1 us
  between operations: 13.5 us -> 0.01 us
  starting transfers between devices: 7.4 us -> 0 us
  local copies, waits for them, and re-layouts: 3.72 us -> 1.38 us
  matrix products: 1.67 us -> 0 us
    reduce_scatter x1 -> x0, waiting for transfers between devices: 54.2 us -> none  [local(): lax.psum_scatter(partial_terms, 'wide', scatter_dimension=1, tiled=True)]
    pallas_call x0 -> x1, Pallas kernels: none -> 18.1 us  [local(): pl.pallas_call(functools.partial(kernel, planes), out_shape=jax.ShapeDtyp...]
    all_to_all x1 -> x0, starting transfers between devices: 7.36 us -> none  [local(): lax.all_to_all(arranged, 'wide', split_axis=1, concat_axis=1, tiled=True)]
    all_to_all x1 -> x0, waiting for transfers between devices: 7.33 us -> none  [local(): lax.all_to_all(arranged, 'wide', split_axis=1, concat_axis=1, tiled=True)]
    reshape x1 -> x0, local copies, waits for them, and re-layouts: 1.7 us -> none  [local(): arranged = year_slab.reshape(group_rows, readers, columns)]
    dot_general x2 -> x0, matrix products: 1.67 us -> none  [the longest x1 1.04 us: local(): jnp.einsum('rsp,pk->rsk', anomaly, patterns, preferred_element_type=jnp.f...]
  transfers between devices with their start and end apart: 2 -> 0, of which waited for: 2 -> 0; matrix products, arithmetic and copies ran while one was open for 1% -> 0% of each run, Pallas kernels for 0% -> 0%
where the time goes in v1:
time: 19.6 us; the launch traced here: 19.4 us
  Pallas kernels  18.1 us (92%)
  local copies, waits for them, and re-layouts  1.38 us (7%)
    pallas_call x1, Pallas kernels, local(): pl.pallas_call(functools.partial(kernel, planes), out_shape=jax.ShapeDtyp...  18.1 us
    unnamed x1, local copies, waits for them, and re-layouts  1.38 us

profile of v1, /device:TPU:0, one launch (start us, length us, event | category | flops | bytes accessed | tf_op | source)
XLA Modules:
  0.0 19.4 jit_solution(12857416070370407887)
XLA Ops:
  0.0 18.1 %shard_map.55 = f32[32,256]{1,0:T(8,128)} custom-call(s32[16]{0:T(128)} %table_ref.1, bf16[32,4096]{1,0:T(8,128)(2,1)} %y_ref.1, f32[21,256]{1,0:T(8,128)} %c_ref.1, bf16[256,256]{1,0:T(8,128)(2,1)} %p_ref.1, s32[1,256]{1,0:T(1,128)} %bitcast.1), custom_call_target="tpu_custom_call" | custom-call | flops 134217728 | bytes 393216 | tf_op jit(solution)/shard_map/pallas_call | solution.py:175
  18.1 1.4 %copy.7 = f32[32,256]{1,0:T(8,128)} copy(f32[32,256]{1,0:T(8,128)} %shard_map.55) | data formatting | bytes 65536

commit v2 on v1

--- a/solution.py
+++ b/solution.py
@@ -51,8 +51,8 @@
 
 
 def kernel(
-    planes, table_ref, y_ref, c_ref, p_ref, mask_ref, out_ref,
-    craw, mraw, cbuf, cstack, pbuf, ybuf, fit, design, sbuf, rbuf,
+    planes, table_hbm, y_ref, c_ref, p_ref, mask_ref, out_ref,
+    table_ref, cbuf, mbuf, cpad, cstack, pbuf, ybuf, fit, design, sbuf, rbuf,
     local_sem, plane_send, plane_recv, y_send, y_recv, r_send, r_recv,
 ):
     rows, wide_columns = ybuf.shape[1:]
@@ -64,16 +64,28 @@
     core = me + 1 - 2 * (lane % 2)
 
     def at_plane(offset):
-        return ((plane + offset + planes) % planes) * LANES + lane
+        return partner(offset) * LANES + lane
+
+    def partner(offset):
+        swapped, bit = plane, 1
+        while bit < planes:
+            if offset & bit:
+                swapped = swapped + bit - 2 * bit * ((plane // bit) % 2)
+            bit *= 2
+        return swapped
+
+    order = list(range(planes - 1, 0, -1))
 
     def block(which):
         return pl.ds(pl.multiple_of(which * columns, columns), columns)
 
-    c_in = pltpu.make_async_copy(c_ref, craw, local_sem.at[0])
-    m_in = pltpu.make_async_copy(mask_ref, mraw, local_sem.at[1])
+    c_in = pltpu.make_async_copy(c_ref, cbuf.at[lane], local_sem.at[0])
+    m_in = pltpu.make_async_copy(mask_ref, mbuf.at[lane], local_sem.at[1])
     p_in = pltpu.make_async_copy(p_ref, pbuf.at[block(lane)], local_sem.at[2])
     here = pl.ds(pl.multiple_of(plane * wide_columns, wide_columns), wide_columns)
     y_in = pltpu.make_async_copy(y_ref.at[:, here], ybuf.at[0], local_sem.at[3])
+    t_in = pltpu.make_async_copy(table_hbm, table_ref, local_sem.at[4])
+    t_in.start()
     c_in.start()
     m_in.start()
     p_in.start()
@@ -83,13 +95,6 @@
     peers = [side, core] + [at_plane(d) for d in range(1, planes)]
     for peer in peers:
         pl.semaphore_signal(barrier, inc=1, device_id={"wide": peer}, device_id_type=pl.DeviceIdType.MESH)
-
-    c_in.wait()
-    m_in.wait()
-    coeff_row = lax.broadcasted_iota(jnp.int32, craw.shape, 0)
-    land = mraw[...].astype(F32)
-    cbuf[lane] = jnp.zeros(cbuf.shape[1:], F32)
-    cbuf[lane, 0:craw.shape[0], :] = craw[...] * jnp.where(coeff_row < SPLIT, 1.0, land)
 
     pl.semaphore_wait(barrier, len(peers))
 
@@ -100,46 +105,59 @@
         )
 
     p_side = remote(p_ref, pbuf.at[block(lane)], plane_send.at[0], plane_recv.at[0], side)
-    c_side = remote(cbuf.at[lane], cbuf.at[lane], plane_send.at[1], plane_recv.at[1], side)
+    c_side = remote(c_ref, cbuf.at[lane], plane_send.at[1], plane_recv.at[1], side)
+    m_side = remote(mask_ref, mbuf.at[lane], plane_send.at[6], plane_recv.at[6], side)
     p_core = remote(p_ref, pbuf.at[block(lane)], plane_send.at[2], plane_recv.at[2], core)
-    c_core = remote(cbuf.at[lane], cbuf.at[lane], plane_send.at[3], plane_recv.at[3], core)
+    c_core = remote(c_ref, cbuf.at[lane], plane_send.at[3], plane_recv.at[3], core)
+    m_core = remote(mask_ref, mbuf.at[lane], plane_send.at[7], plane_recv.at[7], core)
     other = (lane + 2) % LANES
     p_on = remote(pbuf.at[block(other)], pbuf.at[block(other)], plane_send.at[4], plane_recv.at[4], core)
     c_on = remote(cbuf.at[other], cbuf.at[other], plane_send.at[5], plane_recv.at[5], core)
-    y_out = []
-    for d in range(1, planes):
-        to = (plane + d) % planes
+    m_on = remote(mbuf.at[other], mbuf.at[other], plane_send.at[8], plane_recv.at[8], core)
+    y_out = {}
+    for d in order:
+        to = partner(d)
         there = pl.ds(pl.multiple_of(to * wide_columns, wide_columns), wide_columns)
-        y_out.append(remote(y_ref.at[:, there], ybuf.at[d], y_send.at[d], y_recv.at[d], at_plane(d)))
+        y_out[d] = remote(y_ref.at[:, there], ybuf.at[d], y_send.at[d], y_recv.at[d], at_plane(d))
     c_side.start()
-    for copy in y_out:
+    m_side.start()
+    for copy in y_out.values():
         copy.start()
     p_side.start()
     c_core.start()
+    m_core.start()
     p_core.start()
 
     row = lax.broadcasted_iota(jnp.int32, (rows, 1), 0)
+    t_in.wait()
     for d in range(planes):
-        hour = table_ref[at_plane(-d)] * rows + row
+        hour = table_ref[at_plane(d)] * rows + row
         low, high = design_terms(hour, period)
         design[d * rows:(d + 1) * rows, 0:128] = low
         design[d * rows:(d + 1) * rows, 128:256] = high
     cstack[...] = jnp.zeros(cstack.shape, BF16)
+    cpad[...] = jnp.zeros(cpad.shape, F32)
+    held = cbuf.shape[1]
+    masked = lax.broadcasted_iota(jnp.int32, cbuf.shape[1:], 0) >= SPLIT
 
     c_side.wait_recv()
     c_on.start()
-    c_core.wait_recv()
-    p_side.wait_recv()
-    p_on.start()
-    c_on.wait_recv()
-    zeros = jnp.zeros((8, columns), F32)
+    m_side.wait_recv()
+    m_on.start()
+    for copy in (c_in, m_in):
+        copy.wait()
+    for copy in (c_core, m_core, c_on, m_on):
+        copy.wait_recv()
     for l in range(LANES):
-        c1, c2, c3 = thirds(jnp.concatenate([cbuf[l], zeros], 0))
+        cpad[l, 0:held, :] = cbuf[l] * jnp.where(masked, mbuf[l].astype(F32), 1.0)
+        c1, c2, c3 = thirds(cpad[l])
         at = slice(l * columns, (l + 1) * columns)
         for place, term in enumerate((c1, c2, c3, c1, c2, c1)):
             cstack[place * 32:(place + 1) * 32, at] = term
     fit[...] = jnp.dot(design[...], cstack[...], preferred_element_type=F32)
 
+    p_side.wait_recv()
+    p_on.start()
     p_in.wait()
     p_core.wait_recv()
     p_on.wait_recv()
@@ -150,18 +168,18 @@
 
     y_in.wait()
     total = project(0)
-    r_out = []
-    for d in range(1, planes):
-        y_out[d - 1].wait_recv()
+    r_out = {}
+    for d in order:
+        y_out[d].wait_recv()
         sbuf[d] = project(d).astype(sbuf.dtype)
-        copy = remote(sbuf.at[d], rbuf.at[d], r_send.at[d], r_recv.at[d], at_plane(-d))
+        copy = remote(sbuf.at[d], rbuf.at[d], r_send.at[d], r_recv.at[d], at_plane(d))
         copy.start()
-        r_out.append(copy)
-    for d in range(1, planes):
-        r_out[d - 1].wait_recv()
+        r_out[d] = copy
+    for d in order:
+        r_out[d].wait_recv()
         total = total + rbuf[d].astype(F32)
     out_ref[...] = total
-    for copy in [p_side, c_side, p_core, c_core, p_on, c_on] + y_out + r_out:
+    for copy in [p_side, c_side, m_side, p_core, c_core, m_core, p_on, c_on, m_on] + list(y_out.values()) + list(r_out.values()):
         copy.wait_send()
 
 
@@ -172,15 +190,17 @@
     columns, patterns_held = patterns.shape
     wide_columns = LANES * columns
     hbm = pl.BlockSpec(memory_space=pl.ANY)
+    pin = functools.partial(pltpu.with_memory_space_constraint, memory_space=pltpu.HBM)
     return pl.pallas_call(
         functools.partial(kernel, planes),
         out_shape=jax.ShapeDtypeStruct((rows, patterns_held), F32),
-        in_specs=[pl.BlockSpec(memory_space=pltpu.SMEM), hbm, hbm, hbm, hbm],
+        in_specs=[hbm] * 5,
         out_specs=pl.BlockSpec(memory_space=pltpu.VMEM),
         scratch_shapes=[
-            pltpu.VMEM(harmonic_fit.shape, F32),
-            pltpu.VMEM((1, columns), jnp.int32),
-            pltpu.VMEM((LANES, 24, columns), F32),
+            pltpu.SMEM(reader_table.shape, jnp.int32),
+            pltpu.VMEM((LANES,) + harmonic_fit.shape, F32),
+            pltpu.VMEM((LANES, 1, columns), jnp.int32),
+            pltpu.VMEM((LANES, 32, columns), F32),
             pltpu.VMEM((256, wide_columns), BF16),
             pltpu.VMEM((wide_columns, patterns_held), BF16),
             pltpu.VMEM((planes, rows, wide_columns), BF16),
@@ -188,23 +208,23 @@
             pltpu.VMEM((planes * rows, 256), BF16),
             pltpu.VMEM((planes, rows, patterns_held), BF16),
             pltpu.VMEM((planes, rows, patterns_held), BF16),
-            pltpu.SemaphoreType.DMA((4,)),
-            pltpu.SemaphoreType.DMA((6,)),
-            pltpu.SemaphoreType.DMA((6,)),
+            pltpu.SemaphoreType.DMA((5,)),
+            pltpu.SemaphoreType.DMA((9,)),
+            pltpu.SemaphoreType.DMA((9,)),
             pltpu.SemaphoreType.DMA((planes,)),
             pltpu.SemaphoreType.DMA((planes,)),
             pltpu.SemaphoreType.DMA((planes,)),
             pltpu.SemaphoreType.DMA((planes,)),
         ],
         compiler_params=pltpu.CompilerParams(
-            collective_id=0, has_side_effects=True, vmem_limit_bytes=63 * 1024 * 1024 + 900 * 1024
+            collective_id=0, has_side_effects=True, vmem_limit_bytes=40 * 1024 * 1024
         ),
         cost_estimate=pl.CostEstimate(
             flops=2 * planes * rows * wide_columns * (patterns_held + 256),
             bytes_accessed=2 * rows * readers * columns + 2 * columns * patterns_held,
             transcendentals=0,
         ),
-    )(reader_table, year_slab, harmonic_fit, patterns, land_mask.reshape(1, columns))
+    )(pin(reader_table), pin(year_slab), pin(harmonic_fit), pin(patterns), pin(land_mask.reshape(1, columns)))
 
 
 def solution(mesh):

time: 19.6 us -> 16 us (0.82)
  Pallas kernels: 18.1 us -> 15.3 us
  local copies, waits for them, and re-layouts: 1.38 us -> 0.62 us
    pallas_call x1, Pallas kernels: 18.1 us -> 15.3 us  [local(): pl.pallas_call(functools.partial(kernel, planes), out_shape=jax.ShapeDtyp...]
    unnamed x1, local copies, waits for them, and re-layouts: 1.38 us -> 0.62 us
where the time goes in v2:
time: 16 us; the launch traced here: 15.9 us
  Pallas kernels  15.3 us (96%)
  local copies, waits for them, and re-layouts  0.62 us (4%)
    pallas_call x1, Pallas kernels, local(): pl.pallas_call(functools.partial(kernel, planes), out_shape=jax.ShapeDtyp...  15.3 us
    unnamed x1, local copies, waits for them, and re-layouts  0.62 us

profile of v2, /device:TPU:0, one launch (start us, length us, event | category | flops | bytes accessed | tf_op | source)
XLA Modules:
  0.0 15.9 jit_solution(3674252283775384549)
XLA Ops:
  0.0 15.3 %shard_map.55 = f32[32,256]{1,0:T(8,128)S(1)} custom-call(s32[16]{0:T(128)} %table_hbm.1, bf16[32,4096]{1,0:T(8,128)(2,1)} %y_ref.1, f32[21,256]{1,0:T(8,128)} %c_ref.1, bf16[256,256]{1,0:T(8,128)(2,1)} %p_ref.1, s32[1,256]{1,0:T(1,128)} %bitcast.1), custom_call_target="tpu_custom_call" | custom-call | flops 134217728 | bytes 393216 | tf_op jit(solution)/shard_map/pallas_call | solution.py:194
  15.3 0.6 %copy.7 = f32[32,256]{1,0:T(8,128)} copy(f32[32,256]{1,0:T(8,128)S(1)} %shard_map.55) | data formatting | bytes 65536

commit v3 on v2

--- a/solution.py
+++ b/solution.py
@@ -104,14 +104,19 @@
             device_id={"wide": peer}, device_id_type=pl.DeviceIdType.MESH,
         )
 
-    p_side = remote(p_ref, pbuf.at[block(lane)], plane_send.at[0], plane_recv.at[0], side)
+    halves = [pl.ds(0, columns // 2), pl.ds(columns // 2, columns // 2)]
+
+    def part(which, i):
+        return pl.ds(pl.multiple_of(which * columns + i * (columns // 2), columns // 2), columns // 2)
+
+    p_side = [remote(p_ref.at[halves[i]], pbuf.at[part(lane, i)], plane_send.at[(0, 9)[i]], plane_recv.at[(0, 9)[i]], side) for i in range(2)]
     c_side = remote(c_ref, cbuf.at[lane], plane_send.at[1], plane_recv.at[1], side)
     m_side = remote(mask_ref, mbuf.at[lane], plane_send.at[6], plane_recv.at[6], side)
     p_core = remote(p_ref, pbuf.at[block(lane)], plane_send.at[2], plane_recv.at[2], core)
     c_core = remote(c_ref, cbuf.at[lane], plane_send.at[3], plane_recv.at[3], core)
     m_core = remote(mask_ref, mbuf.at[lane], plane_send.at[7], plane_recv.at[7], core)
     other = (lane + 2) % LANES
-    p_on = remote(pbuf.at[block(other)], pbuf.at[block(other)], plane_send.at[4], plane_recv.at[4], core)
+    p_on = [remote(pbuf.at[part(other, i)], pbuf.at[part(other, i)], plane_send.at[(4, 10)[i]], plane_recv.at[(4, 10)[i]], core) for i in range(2)]
     c_on = remote(cbuf.at[other], cbuf.at[other], plane_send.at[5], plane_recv.at[5], core)
     m_on = remote(mbuf.at[other], mbuf.at[other], plane_send.at[8], plane_recv.at[8], core)
     y_out = {}
@@ -121,9 +126,18 @@
         y_out[d] = remote(y_ref.at[:, there], ybuf.at[d], y_send.at[d], y_recv.at[d], at_plane(d))
     c_side.start()
     m_side.start()
-    for copy in y_out.values():
-        copy.start()
-    p_side.start()
+    p_side[0].start()
+    p_side[1].start()
+    @pl.when(lane % 2 == 0)
+    def _():
+        for d in order:
+            y_out[d].start()
+
+    @pl.when(lane % 2 == 1)
+    def _():
+        for d in reversed(order):
+            y_out[d].start()
+
     c_core.start()
     m_core.start()
     p_core.start()
@@ -134,8 +148,7 @@
         hour = table_ref[at_plane(d)] * rows + row
         low, high = design_terms(hour, period)
         design[d * rows:(d + 1) * rows, 0:128] = low
-        design[d * rows:(d + 1) * rows, 128:256] = high
-    cstack[...] = jnp.zeros(cstack.shape, BF16)
+        design[d * rows:(d + 1) * rows, 128:192] = high[:, 0:64]
     cpad[...] = jnp.zeros(cpad.shape, F32)
     held = cbuf.shape[1]
     masked = lax.broadcasted_iota(jnp.int32, cbuf.shape[1:], 0) >= SPLIT
@@ -144,6 +157,9 @@
     c_on.start()
     m_side.wait_recv()
     m_on.start()
+    for i in range(2):
+        p_side[i].wait_recv()
+        p_on[i].start()
     for copy in (c_in, m_in):
         copy.wait()
     for copy in (c_core, m_core, c_on, m_on):
@@ -156,11 +172,10 @@
             cstack[place * 32:(place + 1) * 32, at] = term
     fit[...] = jnp.dot(design[...], cstack[...], preferred_element_type=F32)
 
-    p_side.wait_recv()
-    p_on.start()
     p_in.wait()
     p_core.wait_recv()
-    p_on.wait_recv()
+    for copy in p_on:
+        copy.wait_recv()
 
     def project(d):
         anomaly = ybuf[d].astype(F32) - fit[d * rows:(d + 1) * rows, :]
@@ -179,7 +194,7 @@
         r_out[d].wait_recv()
         total = total + rbuf[d].astype(F32)
     out_ref[...] = total
-    for copy in [p_side, c_side, m_side, p_core, c_core, m_core, p_on, c_on, m_on] + list(y_out.values()) + list(r_out.values()):
+    for copy in p_side + p_on + [c_side, m_side, p_core, c_core, m_core, c_on, m_on] + list(y_out.values()) + list(r_out.values()):
         copy.wait_send()
 
 
@@ -201,16 +216,16 @@
             pltpu.VMEM((LANES,) + harmonic_fit.shape, F32),
             pltpu.VMEM((LANES, 1, columns), jnp.int32),
             pltpu.VMEM((LANES, 32, columns), F32),
-            pltpu.VMEM((256, wide_columns), BF16),
+            pltpu.VMEM((192, wide_columns), BF16),
             pltpu.VMEM((wide_columns, patterns_held), BF16),
             pltpu.VMEM((planes, rows, wide_columns), BF16),
             pltpu.VMEM((planes * rows, wide_columns), F32),
-            pltpu.VMEM((planes * rows, 256), BF16),
+            pltpu.VMEM((planes * rows, 192), BF16),
             pltpu.VMEM((planes, rows, patterns_held), BF16),
             pltpu.VMEM((planes, rows, patterns_held), BF16),
             pltpu.SemaphoreType.DMA((5,)),
-            pltpu.SemaphoreType.DMA((9,)),
-            pltpu.SemaphoreType.DMA((9,)),
+            pltpu.SemaphoreType.DMA((11,)),
+            pltpu.SemaphoreType.DMA((11,)),
             pltpu.SemaphoreType.DMA((planes,)),
             pltpu.SemaphoreType.DMA((planes,)),
             pltpu.SemaphoreType.DMA((planes,)),

time: 16 us -> 16 us (level)
  no operation moved by 1% of the time
where the time goes in v3:
time: 16 us; the launch traced here: 15.9 us
  Pallas kernels  15.3 us (96%)
  local copies, waits for them, and re-layouts  0.62 us (4%)
    pallas_call x1, Pallas kernels, local(): pl.pallas_call(functools.partial(kernel, planes), out_shape=jax.ShapeDtyp...  15.3 us
    unnamed x1, local copies, waits for them, and re-layouts  0.62 us

profile of v3, /device:TPU:0, one launch (start us, length us, event | category | flops | bytes accessed | tf_op | source)
XLA Modules:
  0.0 15.9 jit_solution(4298671154077683073)
XLA Ops:
  0.0 15.3 %shard_map.55 = f32[32,256]{1,0:T(8,128)S(1)} custom-call(s32[16]{0:T(128)} %table_hbm.1, bf16[32,4096]{1,0:T(8,128)(2,1)} %y_ref.1, f32[21,256]{1,0:T(8,128)} %c_ref.1, bf16[256,256]{1,0:T(8,128)(2,1)} %p_ref.1, s32[1,256]{1,0:T(1,128)} %bitcast.1), custom_call_target="tpu_custom_call" | custom-call | flops 134217728 | bytes 393216 | tf_op jit(solution)/shard_map/pallas_call | solution.py:209
  15.3 0.6 %copy.7 = f32[32,256]{1,0:T(8,128)} copy(f32[32,256]{1,0:T(8,128)S(1)} %shard_map.55) | data formatting | bytes 65536

commit v4 on v3

--- a/solution.py
+++ b/solution.py
@@ -181,8 +181,6 @@
         anomaly = ybuf[d].astype(F32) - fit[d * rows:(d + 1) * rows, :]
         return jnp.dot(anomaly.astype(BF16), pbuf[...], preferred_element_type=F32)
 
-    y_in.wait()
-    total = project(0)
     r_out = {}
     for d in order:
         y_out[d].wait_recv()
@@ -190,6 +188,8 @@
         copy = remote(sbuf.at[d], rbuf.at[d], r_send.at[d], r_recv.at[d], at_plane(d))
         copy.start()
         r_out[d] = copy
+    y_in.wait()
+    total = project(0)
     for d in order:
         r_out[d].wait_recv()
         total = total + rbuf[d].astype(F32)

time: 16 us -> 16 us (level)
  no operation moved by 1% of the time
where the time goes in v4:
time: 16 us; the launch traced here: 15.9 us
  Pallas kernels  15.3 us (96%)
  local copies, waits for them, and re-layouts  0.62 us (4%)
    pallas_call x1, Pallas kernels, local(): pl.pallas_call(functools.partial(kernel, planes), out_shape=jax.ShapeDtyp...  15.3 us
    unnamed x1, local copies, waits for them, and re-layouts  0.62 us

profile of v4, /device:TPU:0, one launch (start us, length us, event | category | flops | bytes accessed | tf_op | source)
XLA Modules:
  0.0 15.9 jit_solution(13818011159109639826)
XLA Ops:
  0.0 15.3 %shard_map.55 = f32[32,256]{1,0:T(8,128)S(1)} custom-call(s32[16]{0:T(128)} %table_hbm.1, bf16[32,4096]{1,0:T(8,128)(2,1)} %y_ref.1, f32[21,256]{1,0:T(8,128)} %c_ref.1, bf16[256,256]{1,0:T(8,128)(2,1)} %p_ref.1, s32[1,256]{1,0:T(1,128)} %bitcast.1), custom_call_target="tpu_custom_call" | custom-call | flops 134217728 | bytes 393216 | tf_op jit(solution)/shard_map/pallas_call | solution.py:209
  15.3 0.6 %copy.7 = f32[32,256]{1,0:T(8,128)} copy(f32[32,256]{1,0:T(8,128)S(1)} %shard_map.55) | data formatting | bytes 65536
